TPU v7x, 32 devices: a whole 2x2x4 slice. The times are simulated.
32 devices in a mesh: groups: 2 (over y), rows: 4 (over z), sub: 2 (over x), cols: 2 (over core).
Axes of the slice: x: 2, y: 2, z: 4, core: 2. Of those that a mesh axis runs over, the one named last changes fastest.
Arguments:
- noise: bfloat16 [16384, 256], P(('groups', 'rows', 'sub'), 'cols'), parts along dimension 0, may hold values from -6 to 6
- bases: bfloat16 [2, 16384, 256], P(None, ('groups', 'rows', 'sub')), parts along dimension 1, may hold values from -0.375 to 0.375
- cores: bfloat16 [6, 256, 256], P('groups'), parts along dimension 0, may hold values from -0.09375 to 0.09375
- self_mob: float32 [16384], P(('groups', 'rows', 'sub')), parts along dimension 0, may hold values from 0.5 to 2
Outputs:
- displace: float32 [16384, 256], P(('groups', 'rows', 'sub'), 'cols'), parts along dimension 0
There are 2 independent parts, one for each index of `groups`. A program takes and returns all parts, laid end to end along the dimension named above; each array names one. Nothing has to cross between parts.
All inputs are finite; a program needn't handle non-finite values.
Results may differ from a plain program's by a relative error of at most 0.0022.
Values may be sent and summed in bfloat16 or wider, within the bound.
A program may use at most 64 MiB of HBM per device.

v0:
```python
import jax
import jax.numpy as jnp
from jax import lax
from jax.sharding import PartitionSpec as P


def from_partner(value, axis, stride):
    mask = 2**stride
    pairs = [(source, source ^ mask) for source in range(lax.axis_size(axis))]
    return lax.ppermute(value, axis, pairs)


def level_terms(noise, bases, cores, first, last, depth):
    picked = bases[first:last]
    proj = jnp.einsum("lrk,rc->lck", picked, noise, preferred_element_type=jnp.float32)
    proj = lax.psum(proj, "sub")
    for bit in range(depth - (first + 1)):
        count = min(last, depth - bit - 1) - first
        upper = proj
        merged = upper + from_partner(upper, "rows", bit)
        proj = jnp.concatenate([merged, proj[count:]], axis=0)
    place = lax.axis_index("rows")
    level = first + 1
    bit = depth - level
    node = place // 2**bit
    pair = 2 ** (level - 1) - 1 + node // 2
    core = lax.dynamic_index_in_dim(cores, pair, 0, keepdims=False).astype(jnp.float32)
    odd_node = node % 2 == 1
    sibling_core = jnp.where(odd_node, core, core.T)
    outgoing = jnp.dot(proj[0], sibling_core.T, precision=lax.Precision.HIGHEST).astype(
        jnp.bfloat16
    )
    mapped = from_partner(outgoing, "rows", bit)
    mapped_list = [mapped]
    stacked = jnp.stack(mapped_list, axis=0)
    return jnp.einsum("lrk,lck->rc", picked, stacked, preferred_element_type=jnp.float32)


def per_device(noise, bases, cores, self_mob):
    depth = lax.axis_size("rows").bit_length() - 1
    count_levels = bases.shape[0]
    result = self_mob[:, None] * noise.astype(jnp.float32)
    for level in range(count_levels):
        result = result + level_terms(noise, bases, cores, level, level + 1, depth)
    return result


def solution(mesh):
    in_specs = (
        P(("groups", "rows", "sub"), "cols"),
        P(None, ("groups", "rows", "sub"), None),
        P("groups", None, None),
        P(("groups", "rows", "sub")),
    )
    out_specs = P(("groups", "rows", "sub"), "cols")
    return jax.shard_map(
        per_device, mesh=mesh, in_specs=in_specs, out_specs=out_specs, check_vma=False
    )
```

profile of v0, /device:TPU:0, one launch (start us, length us, event | category | flops | bytes accessed | tf_op | source)
XLA Modules:
  0.0 57.4 jit_solution(1621303815622652117)
XLA Ops:
  6.5 0.0 copy-start.1
  6.5 0.0 all-reduce.3.cloned.1.call-start
  6.5 2.1 %convolution_bitcast_fusion.2 = f32[1,128,256]{2,1,0:T(8,128)} fusion(bf16[1024,128]{1,0:T(8,128)(2,1)} %param.4, bf16[2,1024,256]{2,1,0:T(8,128)(2,1)} %param.5), kind=kOutput, calls=%fused_computation.4 | convolution fusion | flops 67108864 | bytes 917504 | tf_op jit(solution)/shard_map/lrk,rc->lck/dot_general | solution.py:15
  8.6 0.0 copy-done.1
  8.6 2.0 %fusion.3 = f32[128,256]{1,0:T(8,128)} fusion(bf16[1024,128]{1,0:T(8,128)(2,1)S(1)} %copy-done.1, bf16[2,1024,256]{2,1,0:T(8,128)(2,1)} %param.5), kind=kOutput, calls=%fused_computation.8 | convolution fusion | flops 67108864 | bytes 917504 | tf_op jit(solution)/shard_map/lrk,rc->lck/dot_general | solution.py:15
  10.6 0.0 copy-start.2
  10.6 0.0 all-reduce.3.cloned.1.call-update
  10.7 0.1 copy.5
  10.8 0.7 %copy-done.2 = bf16[3,256,256]{2,1,0:T(8,128)(2,1)S(1)} copy-done((bf16[3,256,256]{2,1,0:T(8,128)(2,1)S(1)}, bf16[3,256,256]{2,1,0:T(8,128)(2,1)}, u32[]{:S(2)}) %copy-start.2) | copy-done | bytes 393240
  11.6 0.1 copy.6
  11.8 0.0 copy-start
  11.8 0.1 copy.7
  11.9 24.9 %all-reduce.3.cloned.1.call-done = (f32[128,256]{1,0:T(8,128)}, f32[1,128,256]{2,1,0:T(8,128)}) async-done(((f32[128,256]{1,0:T(8,128)}, f32[1,128,256]{2,1,0:T(8,128)}), (f32[128,256]{1,0:T(8,128)}, f32[1,128,256]{2,1,0:T(8,128)})) %all-reduce.3.cloned.1.call-update) | async-done | bytes 262160 | tf_op jit(solution)/shard_map/psum | solution.py:16
  36.8 1.5 %collective-permute-start = (f32[1,128,256]{2,1,0:T(8,128)}, f32[1,128,256]{2,1,0:T(8,128)S(1)}, u32[]{:S(2)}, u32[]{:S(2)}) collective-permute-start(f32[1,128,256]{2,1,0:T(8,128)} %get-tuple-element.6), channel_id=1, source_target_pairs={{0,4},{4,0},{8,12},{12,8},{1,5},{5,1},{9,13},{13,9},{2,6},{6,2},{1... | collective-permute-start | bytes 393224 | tf_op jit(solution)/shard_map/ppermute | solution.py:10
  38.3 1.3 %convolution_convert_fusion = bf16[128,256]{1,0:T(8,128)(2,1)S(1)} fusion(f32[128,256]{1,0:T(8,128)} %get-tuple-element.5, f32[256,256]{0,1:T(8,128)S(1)} %copy.7, pred[]{:T(512)S(6)} %eq.10, bf16[3,256,256]{2,1,0:T(8,128)(2,1)S(1)} %copy-done.2, s32[]{:T(128)S(6)} %select_n.49), kind=kOutput, calls=%fused_computation.5 | convolution fusion | flops 100827136 | bytes 589829 | tf_op jit(solution)/shard_map/dot_general | solution.py:30
  39.6 0.6 %collective-permute-start.2 = (bf16[128,256]{1,0:T(8,128)(2,1)S(1)}, bf16[128,256]{1,0:T(8,128)(2,1)S(1)}, u32[]{:S(2)}, u32[]{:S(2)}) collective-permute-start(bf16[128,256]{1,0:T(8,128)(2,1)S(1)} %convolution_convert_fusion), channel_id=1, source_target_pairs={{0,4},{4,0},{8,12},{12,8},{1,5},{5,1},{9,13},{13,9},{2,6},{6,2},{1... | collective-permute-start | bytes 196616 | tf_op jit(solution)/shard_map/ppermute | solution.py:10
  40.2 2.4 %collective-permute-done = f32[1,128,256]{2,1,0:T(8,128)S(1)} collective-permute-done((f32[1,128,256]{2,1,0:T(8,128)}, f32[1,128,256]{2,1,0:T(8,128)S(1)}, u32[]{:S(2)}, u32[]{:S(2)}) %collective-permute-start) | collective-permute-done | bytes 131104 | tf_op jit(solution)/shard_map/ppermute | solution.py:10
  42.6 1.3 %convolution_convert_fusion.1 = bf16[128,256]{1,0:T(8,128)(2,1)S(1)} fusion(f32[256,256]{0,1:T(8,128)S(1)} %copy.6, f32[1,128,256]{2,1,0:T(8,128)} %get-tuple-element.6, f32[1,128,256]{2,1,0:T(8,128)S(1)} %collective-permute-done, pred[]{:T(512)S(6)} %eq.9, bf16[3,256,256]{2,1,0:T(8,128)(2,1)S(1)} %copy-done.2, s32[]{:T(128)S(6)} %select_n.45), kind=kOutput, calls=%fused_computation.6 | convolution fusion | flops 100859904 | bytes 720901 | tf_op jit(solution)/shard_map/dot_general | solution.py:30
  44.0 0.0 copy-start.3
  44.0 2.5 %collective-permute-start.1 = (bf16[128,256]{1,0:T(8,128)(2,1)S(1)}, bf16[128,256]{1,0:T(8,128)(2,1)S(1)}, u32[]{:S(2)}, u32[]{:S(2)}) collective-permute-start(bf16[128,256]{1,0:T(8,128)(2,1)S(1)} %convolution_convert_fusion.1), channel_id=1, source_target_pairs={{0,8},{4,12},{8,0},{12,4},{1,9},{5,13},{9,1},{13,5},{2,10},{6,14},... | collective-permute-start | bytes 196616 | tf_op jit(solution)/shard_map/ppermute | solution.py:10
  46.4 0.0 collective-permute-done.2
  46.5 0.0 copy-done
  46.5 0.3 convolution_bitcast_fusion
  46.8 2.4 %collective-permute-done.1 = bf16[128,256]{1,0:T(8,128)(2,1)S(1)} collective-permute-done((bf16[128,256]{1,0:T(8,128)(2,1)S(1)}, bf16[128,256]{1,0:T(8,128)(2,1)S(1)}, u32[]{:S(2)}, u32[]{:S(2)}) %collective-permute-start.1) | collective-permute-done | bytes 65568 | tf_op jit(solution)/shard_map/ppermute | solution.py:10
  49.2 0.0 copy-done.3
  49.2 0.3 fusion.1
  49.5 1.0 %copy.8 = f32[1024,128]{1,0:T(8,128)} copy(f32[1024,128]{0,1:T(8,128)S(1)} %fusion.1) | data formatting | bytes 1048576 | tf_op jit(solution)/shard_map/add | solution.py:44
  (1 shorter events, 0.0 us)
Async XLA Ops:
  6.5 2.1 %copy-start.1 = (bf16[1024,128]{1,0:T(8,128)(2,1)S(1)}, bf16[1024,128]{1,0:T(8,128)(2,1)}, u32[]{:S(2)}) copy-start(bf16[1024,128]{1,0:T(8,128)(2,1)} %param.4) | copy-start | bytes 786436
  6.5 30.3 %all-reduce.3.cloned.1.call-start = ((), (), s32[]{:S(2)}) async-start(), calls=%async_computation | async-start | bytes 524288 | tf_op jit(solution)/shard_map/psum | solution.py:16
  10.6 1.0 %copy-start.2 = (bf16[3,256,256]{2,1,0:T(8,128)(2,1)S(1)}, bf16[3,256,256]{2,1,0:T(8,128)(2,1)}, u32[]{:S(2)}) copy-start(bf16[3,256,256]{2,1,0:T(8,128)(2,1)} %param.6) | copy-start | bytes 1179652
  11.8 34.7 %copy-start = (bf16[2,1024,256]{2,1,0:T(8,128)(2,1)S(1)}, bf16[2,1024,256]{2,1,0:T(8,128)(2,1)}, u32[]{:S(2)}) copy-start(bf16[2,1024,256]{2,1,0:T(8,128)(2,1)} %param.5) | copy-start | bytes 3145732
  36.8 5.8 %collective-permute-start = (f32[1,128,256]{2,1,0:T(8,128)}, f32[1,128,256]{2,1,0:T(8,128)S(1)}, u32[]{:S(2)}, u32[]{:S(2)}) collective-permute-start(f32[1,128,256]{2,1,0:T(8,128)} %get-tuple-element.6), channel_id=1, source_target_pairs={{0,4},{4,0},{8,12},{12,8},{1,5},{5,1},{9,13},{13,9},{2,6},{6,2},{1... | collective-permute-start | bytes 393224 | tf_op jit(solution)/shard_map/ppermute | solution.py:10
  39.6 6.8 %collective-permute-start.2 = (bf16[128,256]{1,0:T(8,128)(2,1)S(1)}, bf16[128,256]{1,0:T(8,128)(2,1)S(1)}, u32[]{:S(2)}, u32[]{:S(2)}) collective-permute-start(bf16[128,256]{1,0:T(8,128)(2,1)S(1)} %convolution_convert_fusion), channel_id=1, source_target_pairs={{0,4},{4,0},{8,12},{12,8},{1,5},{5,1},{9,13},{13,9},{2,6},{6,2},{1... | collective-permute-start | bytes 196616 | tf_op jit(solution)/shard_map/ppermute | solution.py:10
  44.0 5.2 %copy-start.3 = (f32[1024]{0:T(1024)S(1)}, f32[1024]{0:T(1024)}, u32[]{:S(2)}) copy-start(f32[1024]{0:T(1024)} %param.7) | copy-start | bytes 12292
  44.0 5.2 %collective-permute-start.1 = (bf16[128,256]{1,0:T(8,128)(2,1)S(1)}, bf16[128,256]{1,0:T(8,128)(2,1)S(1)}, u32[]{:S(2)}, u32[]{:S(2)}) collective-permute-start(bf16[128,256]{1,0:T(8,128)(2,1)S(1)} %convolution_convert_fusion.1), channel_id=1, source_target_pairs={{0,8},{4,12},{8,0},{12,4},{1,9},{5,13},{9,1},{13,5},{2,10},{6,14},... | collective-permute-start | bytes 196616 | tf_op jit(solution)/shard_map/ppermute | solution.py:10
Sparse Core Ops, SparseCore 0:
  10.7 26.0 all-reduce.2
where the time goes:
time: 57.6 us; the launch traced here: 57.4 us
  waiting for transfers between devices  29.8 us (52%)
  between operations  13.6 us (24%)
  matrix products  7.27 us (13%)
  starting transfers between devices  4.57 us (8%)
  local copies, waits for them, and re-layouts  2.15 us (4%)
    psum x1, waiting for transfers between devices, level_terms(): proj = lax.psum(proj, 'sub')  24.9 us
    ppermute x3, waiting for transfers between devices, from_partner(): return lax.ppermute(value, axis, pairs)  4.87 us
    ppermute x3, starting transfers between devices, from_partner(): return lax.ppermute(value, axis, pairs)  4.57 us
    dot_general x2, matrix products, level_terms(): jnp.einsum('lrk,rc->lck', picked, noise, preferred_element_type=jnp.float32)  4.05 us
    dot_general x2, matrix products, level_terms(): jnp.dot(proj[0], sibling_core.T, precision=lax.Precision.HIGHEST)  2.61 us
  transfers between devices with their start and end apart: 4, of which 3 were waited for; matrix products, arithmetic and copies ran while one was open for 6% of the time, Pallas kernels for 0%

commit v1 on v0

v1 whole, which is shorter than its diff:
```python
import functools

import jax
import jax.numpy as jnp
from jax import lax
from jax.experimental import pallas as pl
from jax.experimental.pallas import tpu as pltpu
from jax.sharding import PartitionSpec as P

MIN_SLICE = 16
MESH = pl.DeviceIdType.MESH
NT = (((1,), (1,)), ((), ()))
NN = (((1,), (0,)), ((), ()))


def flip(index, mask):
    bit = 1
    while bit <= mask:
        if mask & bit:
            index = index + bit * (1 - 2 * (lax.div(index, bit) % 2))
        bit *= 2
    return index


def plan(rows, sub, width, levels):
    out = []
    for level in range(1, levels + 1):
        group = rows // 2 ** (level - 1) * sub
        reducers = min(group, width // MIN_SLICE)
        out.append((group, reducers, width // reducers))
    return out


def halves(value):
    first = value.astype(jnp.bfloat16)
    rest = value - first.astype(jnp.float32)
    second = rest.astype(jnp.bfloat16)
    third = (rest - second.astype(jnp.float32)).astype(jnp.bfloat16)
    return jnp.concatenate([first, second, third], axis=0)


def kernel(rows, sub, levels, block, refs_per_level, *refs):
    noise_hbm, bases_hbm, cores_hbm, mob_ref, out_hbm = refs[:5]
    noise_v, bases_v, cores_v, turned, total, in_sem, base_sem, core_sem, out_sem = refs[5:14]
    per_level = [
        refs[14 + refs_per_level * l : 14 + refs_per_level * (l + 1)] for l in range(levels)
    ]
    beads, width = noise_v.shape
    row, half = lax.axis_index("rows"), lax.axis_index("sub")
    place = row * sub + half
    sizes = plan(rows, sub, width, levels)

    def device(position):
        return {"rows": lax.div(position, sub), "sub": position % sub}

    load_noise = pltpu.make_async_copy(noise_hbm, noise_v, in_sem)
    load_noise.start()
    loads = []
    for l in range(levels):
        loads.append(pltpu.make_async_copy(bases_hbm.at[l], bases_v.at[l], base_sem.at[l]))
        loads[-1].start()
    core_loads = []
    for l in range(levels):
        pair = 2**l - 1 + lax.div(row, rows // 2**l)
        core_loads.append(
            pltpu.make_async_copy(cores_hbm.at[pair], cores_v.at[l], core_sem.at[l])
        )
        core_loads[-1].start()

    barrier = pltpu.get_barrier_semaphore()
    everyone = rows * sub
    for mask in range(1, everyone):
        pl.semaphore_signal(
            barrier, inc=1, device_id=device(flip(place, mask)), device_id_type=MESH
        )

    load_noise.wait()
    for start in range(0, beads, block):
        turned[:, start : start + block] = noise_v[start : start + block, :].T

    sent = []
    for l in range(levels):
        group, reducers, cut = sizes[l]
        proj, got, _, _, send_sem, got_sem, _, _ = per_level[l]
        loads[l].wait()
        part = None
        for start in range(0, beads, block):
            term = lax.dot_general(
                turned[:, start : start + block],
                bases_v[l, start : start + block, :],
                NN,
                preferred_element_type=jnp.float32,
            )
            part = term if part is None else part + term
        proj[...] = part
        if l == 0:
            pl.semaphore_wait(barrier, everyone - 1)
        inner = place % group
        start_of_group = place - inner
        low = inner % reducers
        high = lax.div(inner, reducers)
        copies = []
        for mask in reversed(range(reducers)):
            target = flip(low, mask)
            copy = pltpu.make_async_remote_copy(
                src_ref=proj.at[pl.ds(pl.multiple_of(target * cut, cut), cut)],
                dst_ref=got.at[high * reducers + mask if group > reducers else mask],
                send_sem=send_sem.at[mask],
                recv_sem=got_sem.at[high * reducers + mask if group > reducers else mask],
                device_id=device(start_of_group + target),
                device_id_type=MESH,
            )
            if mask > 0:
                copy.start()
            elif group > reducers:
                pl.when(high > 0)(copy.start)
            copies.append((mask, copy))
        sent.append(copies)

    mob = mob_ref[...].T
    for i in range(beads // 128):
        piece = slice(i * 128, (i + 1) * 128)
        total[piece, :] = mob[:, i : i + 1] * noise_v[piece, :].astype(jnp.float32)

    pending = []
    for l in range(levels):
        group, reducers, cut = sizes[l]
        proj, got, staged, mapped, _, got_sem, z_send, z_sem = per_level[l]
        inner = place % group
        start_of_group = place - inner
        low = inner % reducers
        high = lax.div(inner, reducers)
        own_rows = pl.ds(pl.multiple_of(low * cut, cut), cut)
        even = inner < group // 2
        core_loads[l].wait()

        def reduce(l=l, group=group, reducers=reducers, cut=cut, proj=proj, got=got,
                   staged=staged, mapped=mapped, got_sem=got_sem, z_send=z_send, z_sem=z_sem,
                   inner=inner, start_of_group=start_of_group, low=low, own_rows=own_rows, even=even):
            for slot in range(1, group):
                pltpu.make_async_copy(got.at[slot], got.at[slot], got_sem.at[slot]).wait()
            same = proj[own_rows, :]
            for slot in range(1, group // 2):
                same = same + got[slot]
            other = got[group // 2]
            for slot in range(group // 2 + 1, group):
                other = other + got[slot]
            core = cores_v[l]
            on_even = jnp.where(even, same, other)
            on_odd = jnp.where(even, other, same)
            for_even = lax.dot_general(halves(on_odd), core, NT, preferred_element_type=jnp.float32)
            for_odd = lax.dot_general(halves(on_even), core, NN, preferred_element_type=jnp.float32)
            for_even = for_even[2 * cut :] + for_even[cut : 2 * cut] + for_even[:cut]
            for_odd = for_odd[2 * cut :] + for_odd[cut : 2 * cut] + for_odd[:cut]
            mine = jnp.where(even, for_even, for_odd).astype(jnp.bfloat16)
            theirs = jnp.where(even, for_odd, for_even).astype(jnp.bfloat16)
            staged[0] = mine
            staged[1] = theirs
            mapped[own_rows, :] = mine
            copies = []
            for mask in reversed(range(1, group)):
                copy = pltpu.make_async_remote_copy(
                    src_ref=staged.at[0 if mask < group // 2 else 1],
                    dst_ref=mapped.at[own_rows],
                    send_sem=z_send.at[mask],
                    recv_sem=z_sem.at[mask % reducers],
                    device_id=device(start_of_group + flip(inner, mask)),
                    device_id_type=MESH,
                )
                copy.start()
                copies.append(copy)
            if group > reducers:
                for copy in copies:
                    copy.wait_send()
            return copies

        if group > reducers:
            @pl.when(high == 0)
            def _(reduce=reduce):
                reduce()
        else:
            pending += reduce()

    for l in reversed(range(levels)):
        group, reducers, cut = sizes[l]
        _, _, _, mapped, send_sem, _, _, z_sem = per_level[l]
        inner = place % group
        low = inner % reducers
        high = lax.div(inner, reducers)
        for mask in range(reducers):
            source = flip(low, mask)
            piece = mapped.at[pl.ds(pl.multiple_of(source * cut, cut), cut)]
            arrived = pltpu.make_async_copy(piece, piece, z_sem.at[mask])
            if mask > 0:
                arrived.wait()
            elif group > reducers:
                pl.when(high > 0)(arrived.wait)
        for start in range(0, beads, block):
            piece = slice(start, start + block)
            total[piece, :] += lax.dot_general(
                bases_v[l, piece, :], mapped[...], NT, preferred_element_type=jnp.float32
            )
            if l == 0:
                pltpu.make_async_copy(
                    total.at[piece], out_hbm.at[piece], out_sem.at[start // block]
                ).start()
    for l in range(levels):
        group, reducers, _ = sizes[l]
        high = lax.div(place % group, reducers)
        for mask, copy in sent[l]:
            if mask > 0:
                copy.wait_send()
            elif group > reducers:
                pl.when(high > 0)(copy.wait_send)
    for copy in pending:
        copy.wait_send()
    for start in range(0, beads, block):
        piece = slice(start, start + block)
        pltpu.make_async_copy(
            total.at[piece], out_hbm.at[piece], out_sem.at[start // block]
        ).wait()


def per_device(noise, bases, cores, self_mob):
    rows, sub = lax.axis_size("rows"), lax.axis_size("sub")
    levels, beads, rank = bases.shape
    width = noise.shape[1]
    block = min(beads, 512)
    scratch = [
        pltpu.VMEM((beads, width), noise.dtype),
        pltpu.VMEM(bases.shape, bases.dtype),
        pltpu.VMEM((levels, rank, rank), cores.dtype),
        pltpu.VMEM((width, beads), noise.dtype),
        pltpu.VMEM((beads, width), jnp.float32),
        pltpu.SemaphoreType.DMA(()),
        pltpu.SemaphoreType.DMA((levels,)),
        pltpu.SemaphoreType.DMA((levels,)),
        pltpu.SemaphoreType.DMA((beads // block,)),
    ]
    for group, reducers, cut in plan(rows, sub, width, levels):
        scratch += [
            pltpu.VMEM((width, rank), jnp.float32),
            pltpu.VMEM((group, cut, rank), jnp.float32),
            pltpu.VMEM((2, cut, rank), jnp.bfloat16),
            pltpu.VMEM((width, rank), jnp.bfloat16),
            pltpu.SemaphoreType.DMA((reducers,)),
            pltpu.SemaphoreType.DMA((group,)),
            pltpu.SemaphoreType.DMA((group,)),
            pltpu.SemaphoreType.DMA((reducers,)),
        ]
    return pl.pallas_call(
        functools.partial(kernel, rows, sub, levels, block, 8),
        out_shape=jax.ShapeDtypeStruct((beads, width), jnp.float32),
        in_specs=[pl.BlockSpec(memory_space=pl.ANY)] * 3 + [pl.BlockSpec(memory_space=pltpu.VMEM)],
        out_specs=pl.BlockSpec(memory_space=pl.ANY),
        scratch_shapes=scratch,
        compiler_params=pltpu.CompilerParams(
            collective_id=0, has_side_effects=True, vmem_limit_bytes=40 * 2**20
        ),
    )(noise, bases, cores, self_mob.reshape(beads // 128, 128))


def solution(mesh):
    in_specs = (
        P(("groups", "rows", "sub"), "cols"),
        P(None, ("groups", "rows", "sub"), None),
        P("groups", None, None),
        P(("groups", "rows", "sub")),
    )
    out_specs = P(("groups", "rows", "sub"), "cols")
    return jax.shard_map(
        per_device, mesh=mesh, in_specs=in_specs, out_specs=out_specs, check_vma=False
    )
```

time: 57.6 us -> 21.7 us (0.38)
  waiting for transfers between devices: 29.8 us -> 0 us
  Pallas kernels: 0 us -> 16.7 us
  between operations: 13.6 us -> 0.01 us
  matrix products: 7.27 us -> 0 us
  starting transfers between devices: 4.57 us -> 0 us
  local copies, waits for them, and re-layouts: 2.15 us -> 4.65 us
    psum x1 -> x0, waiting for transfers between devices: 24.9 us -> none  [level_terms(): proj = lax.psum(proj, 'sub')]
    pallas_call x0 -> x1, Pallas kernels: none -> 16.7 us  [per_device(): pl.pallas_call(functools.partial(kernel, rows, sub, levels, block, 8), ou...]
    dot_general x6 -> x0, matrix products: 7.27 us -> none  [the longest x2 4.05 us: level_terms(): jnp.einsum('lrk,rc->lck', picked, noise, preferred_element_type=jnp.float32)]
    ppermute x3 -> x0, waiting for transfers between devices: 4.87 us -> none  [from_partner(): return lax.ppermute(value, axis, pairs)]
    ppermute x3 -> x0, starting transfers between devices: 4.57 us -> none  [from_partner(): return lax.ppermute(value, axis, pairs)]
    unnamed x9, local copies, waits for them, and re-layouts: 0.9 us -> 4.65 us
    add x1 -> x0, local copies, waits for them, and re-layouts: 1 us -> none  [per_device(): result = result + level_terms(noise, bases, cores, level, level + 1, depth)]
  transfers between devices with their start and end apart: 4 -> 0, of which waited for: 3 -> 0; matrix products, arithmetic and copies ran while one was open for 6% -> 0% of each run, Pallas kernels for 0% -> 0%
where the time goes in v1:
time: 21.7 us; the launch traced here: 21.4 us
  Pallas kernels  16.7 us (77%)
  local copies, waits for them, and re-layouts  4.65 us (21%)
    pallas_call x1, Pallas kernels, per_device(): pl.pallas_call(functools.partial(kernel, rows, sub, levels, block, 8), ou...  16.7 us
    unnamed x9, local copies, waits for them, and re-layouts  4.65 us

profile of v1, /device:TPU:0, one launch (start us, length us, event | category | flops | bytes accessed | tf_op | source)
XLA Modules:
  0.0 21.4 jit_solution(16131230228262043192)
XLA Ops:
  0.0 0.0 copy-start
  0.0 1.2 %copy-done = bf16[2,1024,256]{2,1,0:T(8,128)(2,1)S(1)} copy-done((bf16[2,1024,256]{2,1,0:T(8,128)(2,1)S(1)}, bf16[2,1024,256]{2,1,0:T(8,128)(2,1)}, u32[]{:S(2)}) %copy-start) | copy-done | bytes 1048600
  1.2 0.0 copy-start.1
  1.2 1.0 %copy-done.1 = bf16[3,256,256]{2,1,0:T(8,128)(2,1)S(1)} copy-done((bf16[3,256,256]{2,1,0:T(8,128)(2,1)S(1)}, bf16[3,256,256]{2,1,0:T(8,128)(2,1)}, u32[]{:S(2)}) %copy-start.1) | copy-done | bytes 393240
  2.2 0.0 copy-start.2
  2.2 0.9 %copy-done.2 = bf16[1024,128]{1,0:T(8,128)(2,1)S(1)} copy-done((bf16[1024,128]{1,0:T(8,128)(2,1)S(1)}, bf16[1024,128]{1,0:T(8,128)(2,1)}, u32[]{:S(2)}) %copy-start.2) | copy-done | bytes 262168
  3.2 0.0 copy-start.3
  3.2 0.7 %copy-done.3 = f32[1024]{0:T(1024)S(1)} copy-done((f32[1024]{0:T(1024)S(1)}, f32[1024]{0:T(1024)}, u32[]{:S(2)}) %copy-start.3) | copy-done | bytes 4120
  3.9 16.7 %shard_map.46 = f32[1024,128]{1,0:T(8,128)S(1)} custom-call(bf16[1024,128]{1,0:T(8,128)(2,1)S(1)} %copy-done.2, bf16[2,1024,256]{2,1,0:T(8,128)(2,1)S(1)} %copy-done, bf16[3,256,256]{2,1,0:T(8,128)(2,1)S(1)} %copy-done.1, f32[8,128]{1,0:T(8,128)S(1)} %bitcast.1), custom_call_target="tpu_custom_call" | custom-call | tf_op jit(solution)/shard_map/pallas_call | solution.py:251
  20.6 0.8 %copy.6 = f32[1024,128]{1,0:T(8,128)} copy(f32[1024,128]{1,0:T(8,128)S(1)} %shard_map.46) | data formatting | bytes 1048576
Async XLA Ops:
  0.0 1.2 %copy-start = (bf16[2,1024,256]{2,1,0:T(8,128)(2,1)S(1)}, bf16[2,1024,256]{2,1,0:T(8,128)(2,1)}, u32[]{:S(2)}) copy-start(bf16[2,1024,256]{2,1,0:T(8,128)(2,1)} %refs_1_.1) | copy-start | bytes 3145732
  1.2 1.0 %copy-start.1 = (bf16[3,256,256]{2,1,0:T(8,128)(2,1)S(1)}, bf16[3,256,256]{2,1,0:T(8,128)(2,1)}, u32[]{:S(2)}) copy-start(bf16[3,256,256]{2,1,0:T(8,128)(2,1)} %refs_2_.1) | copy-start | bytes 1179652
  2.2 0.9 %copy-start.2 = (bf16[1024,128]{1,0:T(8,128)(2,1)S(1)}, bf16[1024,128]{1,0:T(8,128)(2,1)}, u32[]{:S(2)}) copy-start(bf16[1024,128]{1,0:T(8,128)(2,1)} %refs_0_.1) | copy-start | bytes 786436
  3.2 0.7 %copy-start.3 = (f32[1024]{0:T(1024)S(1)}, f32[1024]{0:T(1024)}, u32[]{:S(2)}) copy-start(f32[1024]{0:T(1024)} %param.7) | copy-start | bytes 12292

commit v2 on v1

--- a/solution.py
+++ b/solution.py
@@ -40,8 +40,8 @@
 
 
 def kernel(rows, sub, levels, block, refs_per_level, *refs):
-    noise_hbm, bases_hbm, cores_hbm, mob_ref, out_hbm = refs[:5]
-    noise_v, bases_v, cores_v, turned, total, in_sem, base_sem, core_sem, out_sem = refs[5:14]
+    noise_hbm, bases_hbm, cores_hbm, mob_hbm, total = refs[:5]
+    noise_v, bases_v, cores_v, turned, mob_v, in_sem, base_sem, core_sem, mob_sem = refs[5:14]
     per_level = [
         refs[14 + refs_per_level * l : 14 + refs_per_level * (l + 1)] for l in range(levels)
     ]
@@ -66,6 +66,9 @@
             pltpu.make_async_copy(cores_hbm.at[pair], cores_v.at[l], core_sem.at[l])
         )
         core_loads[-1].start()
+
+    load_mob = pltpu.make_async_copy(mob_hbm, mob_v, mob_sem)
+    load_mob.start()
 
     barrier = pltpu.get_barrier_semaphore()
     everyone = rows * sub
@@ -117,7 +120,8 @@
             copies.append((mask, copy))
         sent.append(copies)
 
-    mob = mob_ref[...].T
+    load_mob.wait()
+    mob = mob_v[...].T
     for i in range(beads // 128):
         piece = slice(i * 128, (i + 1) * 128)
         total[piece, :] = mob[:, i : i + 1] * noise_v[piece, :].astype(jnp.float32)
@@ -200,10 +204,6 @@
             total[piece, :] += lax.dot_general(
                 bases_v[l, piece, :], mapped[...], NT, preferred_element_type=jnp.float32
             )
-            if l == 0:
-                pltpu.make_async_copy(
-                    total.at[piece], out_hbm.at[piece], out_sem.at[start // block]
-                ).start()
     for l in range(levels):
         group, reducers, _ = sizes[l]
         high = lax.div(place % group, reducers)
@@ -214,11 +214,6 @@
                 pl.when(high > 0)(copy.wait_send)
     for copy in pending:
         copy.wait_send()
-    for start in range(0, beads, block):
-        piece = slice(start, start + block)
-        pltpu.make_async_copy(
-            total.at[piece], out_hbm.at[piece], out_sem.at[start // block]
-        ).wait()
 
 
 def per_device(noise, bases, cores, self_mob):
@@ -231,11 +226,11 @@
         pltpu.VMEM(bases.shape, bases.dtype),
         pltpu.VMEM((levels, rank, rank), cores.dtype),
         pltpu.VMEM((width, beads), noise.dtype),
-        pltpu.VMEM((beads, width), jnp.float32),
+        pltpu.VMEM((beads // 128, 128), jnp.float32),
         pltpu.SemaphoreType.DMA(()),
         pltpu.SemaphoreType.DMA((levels,)),
         pltpu.SemaphoreType.DMA((levels,)),
-        pltpu.SemaphoreType.DMA((beads // block,)),
+        pltpu.SemaphoreType.DMA(()),
     ]
     for group, reducers, cut in plan(rows, sub, width, levels):
         scratch += [
@@ -251,13 +246,13 @@
     return pl.pallas_call(
         functools.partial(kernel, rows, sub, levels, block, 8),
         out_shape=jax.ShapeDtypeStruct((beads, width), jnp.float32),
-        in_specs=[pl.BlockSpec(memory_space=pl.ANY)] * 3 + [pl.BlockSpec(memory_space=pltpu.VMEM)],
-        out_specs=pl.BlockSpec(memory_space=pl.ANY),
+        in_specs=[pl.BlockSpec(memory_space=pltpu.HBM)] * 4,
+        out_specs=pl.BlockSpec(memory_space=pltpu.VMEM),
         scratch_shapes=scratch,
         compiler_params=pltpu.CompilerParams(
             collective_id=0, has_side_effects=True, vmem_limit_bytes=40 * 2**20
         ),
-    )(noise, bases, cores, self_mob.reshape(beads // 128, 128))
+    )(*[pltpu.with_memory_space_constraint(x, pltpu.HBM) for x in (noise, bases, cores, self_mob.reshape(beads // 128, 128))])
 
 
 def solution(mesh):

time: 21.7 us -> 16.8 us (0.77)
  local copies, waits for them, and re-layouts: 4.65 us -> 0.8 us
  Pallas kernels: 16.7 us -> 15.8 us
    unnamed x9 -> x1, local copies, waits for them, and re-layouts: 4.65 us -> 0.8 us
    pallas_call x1, Pallas kernels: 16.7 us -> 15.8 us  [per_device(): pl.pallas_call(functools.partial(kernel, rows, sub, levels, block, 8), ou...]
where the time goes in v2:
time: 16.8 us; the launch traced here: 16.6 us
  Pallas kernels  15.8 us (94%)
  local copies, waits for them, and re-layouts  0.8 us (5%)
    pallas_call x1, Pallas kernels, per_device(): pl.pallas_call(functools.partial(kernel, rows, sub, levels, block, 8), ou...  15.8 us
    unnamed x1, local copies, waits for them, and re-layouts  0.8 us

profile of v2, /device:TPU:0, one launch (start us, length us, event | category | flops | bytes accessed | tf_op | source)
XLA Modules:
  0.0 16.6 jit_solution(4711286895528173118)
XLA Ops:
  0.0 15.8 %shard_map.46 = f32[1024,128]{1,0:T(8,128)S(1)} custom-call(bf16[1024,128]{1,0:T(8,128)(2,1)} %refs_0_.1, bf16[2,1024,256]{2,1,0:T(8,128)(2,1)} %refs_1_.1, bf16[3,256,256]{2,1,0:T(8,128)(2,1)} %refs_2_.1, f32[8,128]{1,0:T(8,128)} %bitcast.1), custom_call_target="tpu_custom_call" | custom-call | tf_op jit(solution)/shard_map/pallas_call | solution.py:246
  15.8 0.8 %copy.6 = f32[1024,128]{1,0:T(8,128)} copy(f32[1024,128]{1,0:T(8,128)S(1)} %shard_map.46) | data formatting | bytes 1048576

commit v3 on v2

v3 whole, which is shorter than its diff:
```python
import functools

import jax
import jax.numpy as jnp
from jax import lax
from jax.experimental import pallas as pl
from jax.experimental.pallas import tpu as pltpu
from jax.sharding import PartitionSpec as P

MIN_SLICE = 16
MESH = pl.DeviceIdType.MESH
NT = (((1,), (1,)), ((), ()))
NN = (((1,), (0,)), ((), ()))


def flip(index, mask):
    bit = 1
    while bit <= mask:
        if mask & bit:
            index = index + bit * (1 - 2 * (lax.div(index, bit) % 2))
        bit *= 2
    return index


def plan(rows, sub, width, levels):
    out = []
    for level in range(1, levels + 1):
        group = rows // 2 ** (level - 1) * sub
        reducers = min(group, width // MIN_SLICE)
        out.append((group, reducers, width // reducers))
    return out


def halves(value):
    first = value.astype(jnp.bfloat16)
    rest = value - first.astype(jnp.float32)
    second = rest.astype(jnp.bfloat16)
    third = (rest - second.astype(jnp.float32)).astype(jnp.bfloat16)
    return jnp.concatenate([first, second, third], axis=0)


def kernel(rows, sub, cols, levels, block, refs_per_level, *refs):
    noise_hbm, bases_hbm, cores_hbm, mob_hbm, total = refs[:5]
    noise_v, bases_v, cores_v, turned, mob_v, in_sem, base_sem, core_sem, mob_sem = refs[5:14]
    per_level = [
        refs[14 + refs_per_level * l : 14 + refs_per_level * (l + 1)] for l in range(levels)
    ]
    beads, width = noise_v.shape
    row, half, col = lax.axis_index("rows"), lax.axis_index("sub"), lax.axis_index("cols")
    place = row * sub + half
    last = cols - 1
    on_last = col == last
    sizes = plan(rows, sub, width, levels)

    def device(position, column):
        return {"rows": lax.div(position, sub), "sub": position % sub, "cols": column}

    load_noise = pltpu.make_async_copy(noise_hbm, noise_v, in_sem)
    load_noise.start()
    loads = []
    for l in range(levels):
        loads.append(pltpu.make_async_copy(bases_hbm.at[l], bases_v.at[l], base_sem.at[l]))
        loads[-1].start()

    barrier = pltpu.get_barrier_semaphore()
    chips = rows * sub

    def greet(position, column):
        pl.semaphore_signal(
            barrier, inc=1, device_id=device(position, column), device_id_type=MESH
        )

    @pl.when(on_last)
    def _():
        for mask in range(chips):
            for column in range(last):
                greet(flip(place, mask), column)

    for mask in range(1, chips):
        greet(flip(place, mask), last)
    pl.when(col < last)(lambda: greet(place, last))

    core_loads = []
    for l in range(levels):
        pair = 2**l - 1 + lax.div(row, rows // 2**l)
        core_loads.append(
            pltpu.make_async_copy(cores_hbm.at[pair], cores_v.at[l], core_sem.at[l])
        )
        core_loads[-1].start()
    load_mob = pltpu.make_async_copy(mob_hbm, mob_v, mob_sem)
    load_mob.start()

    load_noise.wait()
    for start in range(0, beads, block):
        turned[:, start : start + block] = noise_v[start : start + block, :].T

    def spot(l):
        group, reducers, cut = sizes[l]
        inner = place % group
        low = inner % reducers
        high = lax.div(inner, reducers)
        own_rows = pl.ds(pl.multiple_of(low * cut, cut), cut)
        return inner, place - inner, low, high, own_rows

    def is_reducer(l):
        group, reducers, _ = sizes[l]
        if group == reducers:
            return on_last
        return jnp.logical_and(on_last, spot(l)[3] == 0)

    def not_reducer(l):
        group, reducers, _ = sizes[l]
        if group == reducers:
            return col < last
        return jnp.logical_or(col < last, spot(l)[3] > 0)

    def partial_copy(l, mask):
        group, reducers, cut = sizes[l]
        proj, got, _, _, send_sem, got_sem, _, _ = per_level[l]
        _, first, low, high, _ = spot(l)
        target = flip(low, mask)
        slot = col * group + high * reducers + mask
        return pltpu.make_async_remote_copy(
            src_ref=proj.at[pl.ds(pl.multiple_of(target * cut, cut), cut)],
            dst_ref=got.at[slot],
            send_sem=send_sem.at[mask],
            recv_sem=got_sem.at[slot],
            device_id=device(first + target, last),
            device_id_type=MESH,
        )

    def mapped_copies(l):
        group, reducers, _ = sizes[l]
        _, _, staged, mapped, _, _, z_send, z_sem = per_level[l]
        inner, first, _, _, own_rows = spot(l)
        return [
            pltpu.make_async_remote_copy(
                src_ref=staged.at[column * 2 + (0 if mask < group // 2 else 1)],
                dst_ref=mapped.at[own_rows],
                send_sem=z_send.at[column * group + mask],
                recv_sem=z_sem.at[mask % reducers],
                device_id=device(first + flip(inner, mask), column),
                device_id_type=MESH,
            )
            for column in range(cols)
            for mask in reversed(range(group))
            if mask > 0 or column < last
        ]

    for l in range(levels):
        reducers = sizes[l][1]
        proj = per_level[l][0]
        loads[l].wait()
        part = None
        for start in range(0, beads, block):
            term = lax.dot_general(
                turned[:, start : start + block],
                bases_v[l, start : start + block, :],
                NN,
                preferred_element_type=jnp.float32,
            )
            part = term if part is None else part + term
        proj[...] = part
        if l == 0:

            @pl.when(on_last)
            def _():
                pl.semaphore_wait(barrier, chips * cols - 1)

            @pl.when(col < last)
            def _():
                pl.semaphore_wait(barrier, chips)

        for mask in reversed(range(1, reducers)):
            partial_copy(l, mask).start()
        pl.when(not_reducer(l))(lambda l=l: partial_copy(l, 0).start())

    load_mob.wait()
    mob = mob_v[...].T
    for i in range(beads // 128):
        piece = slice(i * 128, (i + 1) * 128)
        total[piece, :] = mob[:, i : i + 1] * noise_v[piece, :].astype(jnp.float32)

    for l in range(levels):
        core_loads[l].wait()

        @pl.when(is_reducer(l))
        def _(l=l):
            group, reducers, cut = sizes[l]
            proj, got, staged, mapped, _, got_sem, _, _ = per_level[l]
            inner, _, _, _, own_rows = spot(l)
            even = inner < group // 2
            for slot in range(cols * group):
                if slot != last * group:
                    pltpu.make_async_copy(got.at[slot], got.at[slot], got_sem.at[slot]).wait()
            on_even, on_odd = [], []
            for column in range(cols):
                base = column * group
                same = proj[own_rows, :] if column == last else got[base]
                for slot in range(1, group // 2):
                    same = same + got[base + slot]
                other = got[base + group // 2]
                for slot in range(group // 2 + 1, group):
                    other = other + got[base + slot]
                on_even.append(jnp.where(even, same, other))
                on_odd.append(jnp.where(even, other, same))
            tall = cols * cut

            def times(value, dims):
                terms = lax.dot_general(
                    halves(jnp.concatenate(value, axis=0)),
                    cores_v[l],
                    dims,
                    preferred_element_type=jnp.float32,
                )
                return terms[2 * tall :] + terms[tall : 2 * tall] + terms[:tall]

            for_even, for_odd = times(on_odd, NT), times(on_even, NN)
            mine = jnp.where(even, for_even, for_odd).astype(jnp.bfloat16)
            theirs = jnp.where(even, for_odd, for_even).astype(jnp.bfloat16)
            for column in range(cols):
                staged[column * 2] = mine[column * cut : (column + 1) * cut]
                staged[column * 2 + 1] = theirs[column * cut : (column + 1) * cut]
            for copy in mapped_copies(l):
                copy.start()
            mapped[own_rows, :] = mine[last * cut :]

    for l in reversed(range(levels)):
        group, reducers, cut = sizes[l]
        mapped, z_sem = per_level[l][3], per_level[l][7]
        low = spot(l)[2]
        for mask in range(reducers):
            source = flip(low, mask)
            piece = mapped.at[pl.ds(pl.multiple_of(source * cut, cut), cut)]
            arrived = pltpu.make_async_copy(piece, piece, z_sem.at[mask])
            if mask > 0:
                arrived.wait()
            else:
                pl.when(not_reducer(l))(arrived.wait)
        for start in range(0, beads, block):
            piece = slice(start, start + block)
            total[piece, :] += lax.dot_general(
                bases_v[l, piece, :], mapped[...], NT, preferred_element_type=jnp.float32
            )
    for l in range(levels):
        for mask in range(1, sizes[l][1]):
            partial_copy(l, mask).wait_send()
        pl.when(not_reducer(l))(lambda l=l: partial_copy(l, 0).wait_send())

        @pl.when(is_reducer(l))
        def _(l=l):
            for copy in mapped_copies(l):
                copy.wait_send()


def per_device(noise, bases, cores, self_mob):
    rows, sub, cols = (lax.axis_size(name) for name in ("rows", "sub", "cols"))
    levels, beads, rank = bases.shape
    width = noise.shape[1]
    block = min(beads, 512)
    scratch = [
        pltpu.VMEM((beads, width), noise.dtype),
        pltpu.VMEM(bases.shape, bases.dtype),
        pltpu.VMEM((levels, rank, rank), cores.dtype),
        pltpu.VMEM((width, beads), noise.dtype),
        pltpu.VMEM((beads // 128, 128), jnp.float32),
        pltpu.SemaphoreType.DMA(()),
        pltpu.SemaphoreType.DMA((levels,)),
        pltpu.SemaphoreType.DMA((levels,)),
        pltpu.SemaphoreType.DMA(()),
    ]
    for group, reducers, cut in plan(rows, sub, width, levels):
        scratch += [
            pltpu.VMEM((width, rank), jnp.float32),
            pltpu.VMEM((cols * group, cut, rank), jnp.float32),
            pltpu.VMEM((2 * cols, cut, rank), jnp.bfloat16),
            pltpu.VMEM((width, rank), jnp.bfloat16),
            pltpu.SemaphoreType.DMA((reducers,)),
            pltpu.SemaphoreType.DMA((cols * group,)),
            pltpu.SemaphoreType.DMA((cols * group,)),
            pltpu.SemaphoreType.DMA((reducers,)),
        ]
    return pl.pallas_call(
        functools.partial(kernel, rows, sub, cols, levels, block, 8),
        out_shape=jax.ShapeDtypeStruct((beads, width), jnp.float32),
        in_specs=[pl.BlockSpec(memory_space=pltpu.HBM)] * 4,
        out_specs=pl.BlockSpec(memory_space=pltpu.VMEM),
        scratch_shapes=scratch,
        compiler_params=pltpu.CompilerParams(
            collective_id=0, has_side_effects=True, vmem_limit_bytes=40 * 2**20
        ),
    )(*[pltpu.with_memory_space_constraint(x, pltpu.HBM) for x in (noise, bases, cores, self_mob.reshape(beads // 128, 128))])


def solution(mesh):
    in_specs = (
        P(("groups", "rows", "sub"), "cols"),
        P(None, ("groups", "rows", "sub"), None),
        P("groups", None, None),
        P(("groups", "rows", "sub")),
    )
    out_specs = P(("groups", "rows", "sub"), "cols")
    return jax.shard_map(
        per_device, mesh=mesh, in_specs=in_specs, out_specs=out_specs, check_vma=False
    )
```

time: 16.8 us -> 16.2 us (0.964)
  Pallas kernels: 15.8 us -> 15.3 us
    pallas_call x1, Pallas kernels: 15.8 us -> 15.3 us  [per_device(): pl.pallas_call(functools.partial(kernel, rows, sub, cols, levels, block,...]
where the time goes in v3:
time: 16.2 us; the launch traced here: 16.1 us
  Pallas kernels  15.3 us (94%)
  local copies, waits for them, and re-layouts  0.8 us (5%)
    pallas_call x1, Pallas kernels, per_device(): pl.pallas_call(functools.partial(kernel, rows, sub, cols, levels, block,...  15.3 us
    unnamed x1, local copies, waits for them, and re-layouts  0.8 us

profile of v3, /device:TPU:0, one launch (start us, length us, event | category | flops | bytes accessed | tf_op | source)
XLA Modules:
  0.0 16.1 jit_solution(3215329893589505777)
XLA Ops:
  0.0 15.3 %shard_map.46 = f32[1024,128]{1,0:T(8,128)S(1)} custom-call(bf16[1024,128]{1,0:T(8,128)(2,1)} %refs_0_.1, bf16[2,1024,256]{2,1,0:T(8,128)(2,1)} %refs_1_.1, bf16[3,256,256]{2,1,0:T(8,128)(2,1)} %refs_2_.1, f32[8,128]{1,0:T(8,128)} %bitcast.1), custom_call_target="tpu_custom_call" | custom-call | tf_op jit(solution)/shard_map/pallas_call | solution.py:283
  15.3 0.8 %copy.6 = f32[1024,128]{1,0:T(8,128)} copy(f32[1024,128]{1,0:T(8,128)S(1)} %shard_map.46) | data formatting | bytes 1048576
